TPU v7x, 32 devices: a whole 2x2x4 slice. The times are simulated.
32 devices in a mesh: doc: 4 (over y, core), term: 8 (over z, x).
Axes of the slice: x: 2, y: 2, z: 4, core: 2. Of those that a mesh axis runs over, the one named last changes fastest.
Arguments:
- slab: float32 [4096, 8192], P('doc', 'term'), may hold values from 0.05 to 4
- doc_factor: float32 [4096, 128], P('doc'), may hold values from 0.02 to 5, as said below
- term_factor: float32 [8192, 128], P('term'), may hold values from 0.005 to 5, as said below
Outputs:
- doc_out: float32 [4096, 128], P('doc')
- term_out: float32 [8192, 128], P('term')
Inputs may be any that keep to these rules, and one draw needn't show every extreme that they name: `doc_factor`: positive entries. `term_factor`: positive entries.
All inputs are finite; a program needn't handle non-finite values.
Results may differ from a plain program's by a relative error of at most 0.0001.
Values sent between devices are 32-bit elements; how exact they have to be, the bound alone decides.
A program may use at most 64 MiB of HBM per device.

v0:
```python
import jax
import jax.numpy as jnp
from jax import lax
from jax.sharding import PartitionSpec as P

OUTER = 2
INNER = 2


def quotient(slab, doc_factor, term_factor):
    product = jnp.dot(
        doc_factor,
        term_factor.T,
        precision=lax.Precision.HIGHEST,
        preferred_element_type=jnp.float32,
    )
    return slab / product


def on_device(slab, doc_factor, term_factor):
    for _ in range(OUTER):
        term_mass = lax.psum(jnp.sum(term_factor, axis=0), "term")
        for _ in range(INNER):
            ratios = quotient(slab, doc_factor, term_factor)
            partial_value = jnp.dot(
                ratios,
                term_factor,
                precision=lax.Precision.HIGHEST,
                preferred_element_type=jnp.float32,
            )
            numerator = lax.psum(partial_value, "term")
            doc_factor = doc_factor * numerator / term_mass
        ratios = quotient(slab, doc_factor, term_factor)
        local_terms = jnp.dot(
            ratios.T,
            doc_factor,
            precision=lax.Precision.HIGHEST,
            preferred_element_type=jnp.float32,
        )
        numerator, doc_mass = lax.psum((local_terms, jnp.sum(doc_factor, axis=0)), "doc")
        term_factor = term_factor * numerator / doc_mass
    return (doc_factor, term_factor)


def solution(mesh):
    return jax.shard_map(
        on_device,
        mesh=mesh,
        in_specs=(P("doc", "term"), P("doc", None), P("term", None)),
        out_specs=(P("doc", None), P("term", None)),
        check_vma=False,
    )
```

profile of v0, /device:TPU:0, one launch (start us, length us, event | category | flops | bytes accessed | tf_op | source)
XLA Modules:
  0.0 433.9 jit_solution(8701841157308178894)
XLA Ops:
  7.2 0.0 copy-start
  7.2 0.0 all-reduce.7.cloned.1.call-start
  7.2 0.0 copy-start.5
  7.2 4.8 %fusion.17 = f32[1024,1024]{1,0:T(8,128)S(1)} fusion(f32[1024,128]{1,0:T(8,128)} %param.4, f32[1024,128]{1,0:T(8,128)} %param.5), kind=kOutput, calls=%fused_computation.23 | convolution fusion | flops 1610612736 | bytes 5242880 | tf_op jit(solution)/shard_map/dot_general | solution.py:11
  12.1 0.0 copy-done
  12.1 0.0 copy-done.5
  12.1 0.0 copy-start.1
  12.1 4.3 fusion.10
  16.4 0.0 all-reduce.7.cloned.1.call-update
  16.4 0.0 all-reduce.9.cloned.1.call-start
  16.4 0.1 reduce_sum.36
  16.6 23.5 %psum.71 = f32[128]{0:T(128)S(1)} all-reduce(f32[128]{0:T(128)S(1)} %reduce_sum.36), channel_id=1, replica_groups=mesh['doc'=4,'term'=8] {'term'}, use_global_device_ids=true, to_apply=%region_2.0 | all-reduce | flops 128 | bytes 1024 | tf_op jit(solution)/shard_map/psum | solution.py:22
  40.1 51.5 %all-reduce.7.cloned.1.call-done = f32[1024,128]{1,0:T(8,128)} async-done(((f32[1024,128]{1,0:T(8,128)}), f32[1024,128]{1,0:T(8,128)}) %all-reduce.7.cloned.1.call-update) | async-done | bytes 524304 | tf_op jit(solution)/shard_map/psum | solution.py:31
  91.6 0.0 copy-done.1
  91.6 0.0 copy-start.6
  91.6 4.7 %fusion.12 = f32[1024,1024]{1,0:T(8,128)S(1)} fusion(f32[1024,128]{1,0:T(8,128)S(1)} %copy-done, f32[1024,128]{1,0:T(8,128)S(1)} %copy-done.1, f32[1024,128]{1,0:T(8,128)} %all-reduce.7.cloned.1.call-done, f32[128]{0:T(128)S(1)} %psum.71), kind=kOutput, calls=%fused_computation.18 | convolution fusion | flops 1610874880 | bytes 5767680 | tf_op jit(solution)/shard_map/dot_general | solution.py:11
  96.3 0.0 copy-done.6
  96.3 0.0 copy-start.2
  96.3 4.3 fusion.8
  100.6 0.0 all-reduce.9.cloned.1.call-update
  100.6 0.3 all-reduce.11.cloned.1.call-start
  100.9 71.5 %all-reduce.9.cloned.1.call-done = f32[1024,128]{1,0:T(8,128)} async-done(((f32[1024,128]{1,0:T(8,128)}), f32[1024,128]{1,0:T(8,128)}) %all-reduce.9.cloned.1.call-update) | async-done | bytes 524304 | tf_op jit(solution)/shard_map/psum | solution.py:31
  172.4 0.0 copy-done.2
  172.4 0.0 copy-start.7
  172.4 1.4 fusion.16
  173.8 3.5 fusion.18
  177.3 0.0 copy-done.7
  177.3 7.5 %fusion.6 = f32[1024,128]{1,0:T(8,128)} fusion(f32[1024,128]{1,0:T(8,128)S(1)} %get-tuple-element.7, f32[1024,1024]{1,0:T(8,128)S(1)} %copy-done.7, f32[1024,1024]{1,0:T(8,128)S(1)} %fusion.18), kind=kOutput, calls=%fused_computation.6 | convolution fusion | flops 1611661312 | bytes 9437184 | tf_op jit(solution)/shard_map/dot_general | solution.py:34
  184.8 0.0 all-reduce.11.cloned.1.call-update
  184.9 0.0 all-reduce.13.cloned.1.call-start
  184.9 6.1 %psum.74 = f32[128]{0:T(128)S(1)} all-reduce(f32[128]{0:T(128)S(1)} %get-tuple-element.6), channel_id=1, replica_groups=mesh['doc'=4,'term'=8] {'doc'}, use_global_device_ids=true, to_apply=%region_6.0 | all-reduce | flops 128 | bytes 1024 | tf_op jit(solution)/shard_map/psum | solution.py:40
  191.0 26.4 %all-reduce.11.cloned.1.call-done = f32[1024,128]{1,0:T(8,128)} async-done(((f32[1024,128]{1,0:T(8,128)}), f32[1024,128]{1,0:T(8,128)}) %all-reduce.11.cloned.1.call-update) | async-done | bytes 524304 | tf_op jit(solution)/shard_map/psum | solution.py:40
  217.5 0.0 copy-start.8
  217.5 1.4 fusion.15
  218.8 3.5 fusion.19
  222.3 0.0 copy-done.8
  222.3 4.3 fusion.4
  226.6 0.0 all-reduce.13.cloned.1.call-update
  226.6 0.0 all-reduce.15.cloned.1.call-start
  226.6 21.7 %psum.76 = f32[128]{0:T(128)S(1)} all-reduce(f32[128]{0:T(128)S(1)} %get-tuple-element.4), channel_id=1, replica_groups=mesh['doc'=4,'term'=8] {'term'}, use_global_device_ids=true, to_apply=%region_9.0 | all-reduce | flops 128 | bytes 1024 | tf_op jit(solution)/shard_map/psum | solution.py:22
  248.4 50.8 %all-reduce.13.cloned.1.call-done = f32[1024,128]{1,0:T(8,128)} async-done(((f32[1024,128]{1,0:T(8,128)}), f32[1024,128]{1,0:T(8,128)}) %all-reduce.13.cloned.1.call-update) | async-done | bytes 524304 | tf_op jit(solution)/shard_map/psum | solution.py:31
  299.2 0.0 copy-start.9
  299.2 4.7 %fusion.13 = f32[1024,1024]{1,0:T(8,128)S(1)} fusion(f32[1024,128]{1,0:T(8,128)S(1)} %get-tuple-element.5, f32[1024,128]{1,0:T(8,128)S(1)} %get-tuple-element.7, f32[1024,128]{1,0:T(8,128)} %all-reduce.13.cloned.1.call-done, f32[128]{0:T(128)S(1)} %psum.76), kind=kOutput, calls=%fused_computation.19 | convolution fusion | flops 1610874880 | bytes 5767680 | tf_op jit(solution)/shard_map/dot_general | solution.py:11
  303.9 0.0 copy-done.9
  303.9 0.0 copy-start.3
  303.9 4.3 fusion.2
  308.1 0.0 all-reduce.15.cloned.1.call-update
  308.2 0.3 all-reduce.17.cloned.1.call-start
  308.4 71.6 %all-reduce.15.cloned.1.call-done = f32[1024,128]{1,0:T(8,128)} async-done(((f32[1024,128]{1,0:T(8,128)}), f32[1024,128]{1,0:T(8,128)}) %all-reduce.15.cloned.1.call-update) | async-done | bytes 524304 | tf_op jit(solution)/shard_map/psum | solution.py:31
  380.0 0.0 copy-done.3
  380.0 0.0 copy-start.10
  380.0 1.4 fusion.14
  381.4 0.0 copy-start.4
  381.4 3.5 fusion.20
  384.8 0.0 copy-done.10
  384.9 7.5 %fusion = f32[1024,128]{1,0:T(8,128)} fusion(f32[1024,128]{1,0:T(8,128)S(1)} %get-tuple-element.3, f32[1024,1024]{1,0:T(8,128)S(1)} %copy-done.10, f32[1024,1024]{1,0:T(8,128)S(1)} %fusion.20), kind=kOutput, calls=%fused_computation | convolution fusion | flops 1611661312 | bytes 9437184 | tf_op jit(solution)/shard_map/dot_general | solution.py:34
  392.4 0.0 copy-done.4
  392.4 0.0 all-reduce.17.cloned.1.call-update
  392.4 5.7 %psum.79 = f32[128]{0:T(128)S(1)} all-reduce(f32[128]{0:T(128)S(1)} %get-tuple-element.2), channel_id=1, replica_groups=mesh['doc'=4,'term'=8] {'doc'}, use_global_device_ids=true, to_apply=%region_13.0 | all-reduce | flops 128 | bytes 1024 | tf_op jit(solution)/shard_map/psum | solution.py:40
  398.1 26.8 %all-reduce.17.cloned.1.call-done = f32[1024,128]{1,0:T(8,128)} async-done(((f32[1024,128]{1,0:T(8,128)}), f32[1024,128]{1,0:T(8,128)}) %all-reduce.17.cloned.1.call-update) | async-done | bytes 524304 | tf_op jit(solution)/shard_map/psum | solution.py:40
  424.9 1.9 multiply_divide_fusion
Async XLA Ops:
  7.2 4.9 %copy-start = (f32[1024,128]{1,0:T(8,128)S(1)}, f32[1024,128]{1,0:T(8,128)}, u32[]{:S(2)}) copy-start(f32[1024,128]{1,0:T(8,128)} %param.5) | copy-start | bytes 1572868
  7.2 84.4 %all-reduce.7.cloned.1.call-start = ((), (), s32[]{:S(2)}) async-start(), calls=%async_computation | async-start | bytes 1048576 | tf_op jit(solution)/shard_map/psum | solution.py:31
  7.2 4.9 %copy-start.5 = (f32[1024,1024]{1,0:T(8,128)S(1)}, f32[1024,1024]{1,0:T(8,128)}, u32[]{:S(2)}) copy-start(f32[1024,1024]{1,0:T(8,128)} %param.3) | copy-start | bytes 12582916
  12.1 79.5 %copy-start.1 = (f32[1024,128]{1,0:T(8,128)S(1)}, f32[1024,128]{1,0:T(8,128)}, u32[]{:S(2)}) copy-start(f32[1024,128]{1,0:T(8,128)} %param.4) | copy-start | bytes 1572868
  16.4 156.0 %all-reduce.9.cloned.1.call-start = ((), (), s32[]{:S(2)}) async-start(), calls=%async_computation.1 | async-start | bytes 1048576 | tf_op jit(solution)/shard_map/psum | solution.py:31
  91.6 4.7 %copy-start.6 = (f32[1024,1024]{1,0:T(8,128)S(1)}, f32[1024,1024]{1,0:T(8,128)}, u32[]{:S(2)}) copy-start(f32[1024,1024]{1,0:T(8,128)} %param.3) | copy-start | bytes 12582916
  96.3 76.1 %copy-start.2 = (f32[1024,128]{1,0:T(8,128)S(1)}, f32[1024,128]{1,0:T(8,128)}, u32[]{:S(2)}) copy-start(f32[1024,128]{1,0:T(8,128)} %all-reduce.7.cloned.1.call-done) | copy-start | bytes 1572868
  100.6 116.8 %all-reduce.11.cloned.1.call-start = ((), (), s32[]{:S(2)}) async-start(), calls=%async_computation.2 | async-start | bytes 1048576 | tf_op jit(solution)/shard_map/psum | solution.py:40
  172.4 4.8 %copy-start.7 = (f32[1024,1024]{1,0:T(8,128)S(1)}, f32[1024,1024]{1,0:T(8,128)}, u32[]{:S(2)}) copy-start(f32[1024,1024]{1,0:T(8,128)} %param.3) | copy-start | bytes 12582916
  184.9 114.3 %all-reduce.13.cloned.1.call-start = ((), (), s32[]{:S(2)}) async-start(), calls=%async_computation.3 | async-start | bytes 1048576 | tf_op jit(solution)/shard_map/psum | solution.py:31
  217.5 4.8 %copy-start.8 = (f32[1024,1024]{1,0:T(8,128)S(1)}, f32[1024,1024]{1,0:T(8,128)}, u32[]{:S(2)}) copy-start(f32[1024,1024]{1,0:T(8,128)} %param.3) | copy-start | bytes 12582916
  226.6 153.4 %all-reduce.15.cloned.1.call-start = ((), (), s32[]{:S(2)}) async-start(), calls=%async_computation.4 | async-start | bytes 1048576 | tf_op jit(solution)/shard_map/psum | solution.py:31
  299.2 4.7 %copy-start.9 = (f32[1024,1024]{1,0:T(8,128)S(1)}, f32[1024,1024]{1,0:T(8,128)}, u32[]{:S(2)}) copy-start(f32[1024,1024]{1,0:T(8,128)} %param.3) | copy-start | bytes 12582916
  303.9 76.1 %copy-start.3 = (f32[1024,128]{1,0:T(8,128)S(1)}, f32[1024,128]{1,0:T(8,128)}, u32[]{:S(2)}) copy-start(f32[1024,128]{1,0:T(8,128)} %all-reduce.13.cloned.1.call-done) | copy-start | bytes 1572868
  308.2 116.8 %all-reduce.17.cloned.1.call-start = ((), (), s32[]{:S(2)}) async-start(), calls=%async_computation.5 | async-start | bytes 1048576 | tf_op jit(solution)/shard_map/psum | solution.py:40
  380.0 4.8 %copy-start.10 = (f32[1024,1024]{1,0:T(8,128)S(1)}, f32[1024,1024]{1,0:T(8,128)}, u32[]{:S(2)}) copy-start(f32[1024,1024]{1,0:T(8,128)} %param.3) | copy-start | bytes 12582916
  381.4 11.0 %copy-start.4 = (f32[1024,128]{1,0:T(8,128)}, f32[1024,128]{1,0:T(8,128)S(1)}, u32[]{:S(2)}) copy-start(f32[1024,128]{1,0:T(8,128)S(1)} %get-tuple-element.3) | copy-start | bytes 1572868
Sparse Core Ops, SparseCore 0:
  16.5 75.0 all-reduce.6
  100.7 71.6 all-reduce.8
  185.0 32.4 all-reduce.10
  226.7 72.4 all-reduce.12
  308.3 71.6 all-reduce.14
  392.6 32.3 all-reduce.16
where the time goes:
time: 440 us; the launch traced here: 434 us
  waiting for transfers between devices  299 us (68%)
  blocking collectives  57 us (13%)
  matrix products  56.7 us (13%)
  between operations  14.5 us (3%)
  other arithmetic  6.1 us (1%)
    psum x4, waiting for transfers between devices, on_device(): numerator = lax.psum(partial_value, 'term')  245 us
    psum x2, waiting for transfers between devices, on_device(): lax.psum((local_terms, jnp.sum(doc_factor, axis=0)), 'doc')  53.3 us
    psum x2, blocking collectives, on_device(): term_mass = lax.psum(jnp.sum(term_factor, axis=0), 'term')  45.2 us
    dot_general x6, matrix products, quotient(): jnp.dot(doc_factor, term_factor.T, precision=lax.Precision.HIGHEST, prefe...  24.6 us
    dot_general x4, matrix products, on_device(): jnp.dot(ratios, term_factor, precision=lax.Precision.HIGHEST, preferred_e...  17 us
    dot_general x2, matrix products, on_device(): jnp.dot(ratios.T, doc_factor, precision=lax.Precision.HIGHEST, preferred_...  15.1 us
    psum x2, blocking collectives, on_device(): lax.psum((local_terms, jnp.sum(doc_factor, axis=0)), 'doc')  11.8 us
  transfers between devices with their start and end apart: 6, of which 6 were waited for; matrix products, arithmetic and copies ran while one was open for 0% of the time, Pallas kernels for 0%

commit v1 on v0

v1 whole, which is shorter than its diff:
```python
import functools

import jax
import jax.numpy as jnp
from jax import lax
from jax.experimental import pallas as pl
from jax.experimental.pallas import tpu as pltpu
from jax.sharding import PartitionSpec as P

OUTER = 2
INNER = 2
TILE = 256
DOC_CHUNKS = 4
TERM_CHUNKS = 2
MESH = pl.DeviceIdType.MESH
F32 = jnp.float32
BF16 = jnp.bfloat16


def halves(x):
    high = x.astype(BF16)
    return high, (x - high.astype(F32)).astype(BF16)


def dot(a, b, dims=((1,), (0,))):
    return lax.dot_general(a, b, (dims, ((), ())), preferred_element_type=F32)


def fold(x):
    rows, cols = x.shape
    return jnp.sum(x.reshape(rows // 8, 8, cols), axis=0)


class Group:
    def __init__(self, axis, size):
        self.axis, self.size = axis, size
        self.outer = size // 2
        self.me = lax.axis_index(axis)
        self.x = lax.rem(self.me, 2)
        self.z = lax.div(self.me, 2)
        self.pair = {axis: self.me + 1 - 2 * self.x}

    def place(self, d):
        return lax.rem(self.z + d, self.outer)

    def peer(self, d):
        return {self.axis: self.place(d) * 2 + self.x}

    def everyone(self):
        return [self.pair] + [self.peer(d) for d in range(1, self.outer)]


class Reduce:
    def __init__(self, group, rows, part, r1, acc, r2, send, recv):
        self.g, self.rows = group, rows
        self.half, self.own = rows // 2, rows // 2 // group.outer
        self.part, self.r1, self.acc, self.r2 = part, r1, acc, r2
        self.send, self.recv = send, recv

    def copy(self, src, dst, stage, device):
        return pltpu.make_async_remote_copy(
            src_ref=src, dst_ref=dst, send_sem=self.send.at[stage], recv_sem=self.recv.at[stage],
            device_id=device, device_id_type=MESH)

    def many(self, sem):
        pltpu.make_async_copy(self.r2, self.r2, sem).wait()

    def half_at(self, x):
        return pl.multiple_of(x * self.half, 8)

    def s1(self):
        self.c1 = self.copy(self.part.at[pl.ds(self.half_at(1 - self.g.x), self.half)], self.r1, 0, self.g.pair)
        self.c1.start()

    def s2(self):
        self.c1.wait()
        self.acc[...] = self.part[pl.ds(self.half_at(self.g.x), self.half)] + self.r1[...]
        for d in range(1, self.g.outer):
            at = pl.multiple_of(self.g.place(d) * self.own, 8)
            self.copy(self.acc.at[pl.ds(at, self.own)], self.r2.at[d - 1], 1, self.g.peer(d)).start()

    def s3(self, base, old, new, mass):
        self.new, self.base = new, base
        if self.g.outer > 1:
            self.many(self.recv.at[1])
        total = self.acc[pl.ds(pl.multiple_of(self.g.z * self.own, 8), self.own)]
        for d in range(self.g.outer - 1):
            total = total + self.r2[d]
        at = pl.multiple_of(base + self.half_at(self.g.x) + self.g.z * self.own, 8)
        rows = pl.ds(at, self.own)
        new[rows] = old[rows] * total / mass()
        for d in range(1, self.g.outer):
            self.copy(new.at[rows], new.at[rows], 2, self.g.peer(d)).start()

    def s4(self):
        if self.g.outer > 1:
            self.many(self.recv.at[2])
            self.many(self.send.at[1])
        rows = pl.ds(pl.multiple_of(self.base + self.half_at(self.g.x), 8), self.half)
        self.c4 = self.copy(self.new.at[rows], self.new.at[rows], 3, self.g.pair)
        self.c4.start()

    def s5(self):
        self.c4.wait()
        if self.g.outer > 1:
            self.many(self.send.at[2])


class Mass:
    def __init__(self, group, buf, got, send, recv):
        self.g, self.buf, self.got, self.send, self.recv = group, buf, got, send, recv

    def copy(self, src, dst, stage, device):
        return pltpu.make_async_remote_copy(
            src_ref=src, dst_ref=dst, send_sem=self.send.at[stage], recv_sem=self.recv.at[stage],
            device_id=device, device_id_type=MESH)

    def s1(self, value):
        self.buf[0] = value
        self.c1 = self.copy(self.buf.at[0], self.got.at[0], 0, self.g.pair)
        self.c1.start()

    def s2(self):
        self.c1.wait()
        self.buf[1] = self.buf[0] + self.got[0]
        for d in range(1, self.g.outer):
            self.copy(self.buf.at[1], self.got.at[d], 1, self.g.peer(d)).start()

    def s3(self):
        total = self.buf[1]
        if self.g.outer > 1:
            rest = self.got.at[pl.ds(1, self.g.outer - 1)]
            pltpu.make_async_copy(rest, rest, self.recv.at[1]).wait()
            pltpu.make_async_copy(rest, rest, self.send.at[1]).wait()
            for d in range(1, self.g.outer):
                total = total + self.got[d]
        self.buf[2] = jnp.broadcast_to(jnp.sum(total, axis=0, keepdims=True), total.shape)

    def value(self):
        return self.buf[2, 0:1]


def kernel(docs_axis, terms_axis, slab, h_in, w_in, h_out, w_out,
           hbuf, wbuf, wk, tt,
           dpart, dr1, dacc, dr2, dsend, drecv,
           tpart, tr1, tacc, tr2, tsend, trecv,
           mbuf, mgot, msend, mrecv, cbuf, cgot, csend, crecv):
    docs, terms = slab.shape
    rank = h_in.shape[1]
    gt, gd = Group(*terms_axis), Group(*docs_axis)
    peers = gt.everyone() + gd.everyone()
    barrier = pltpu.get_barrier_semaphore()
    for device in peers:
        pl.semaphore_signal(barrier, inc=1, device_id=device, device_id_type=MESH)
    pl.semaphore_wait(barrier, len(peers))

    chunk, tchunk = docs // DOC_CHUNKS, terms // TERM_CHUNKS
    tile = min(TILE, terms)

    def quotients(h, rows):
        high, low = halves(h)
        lhs = jnp.concatenate([high, low, high], axis=1)
        for t in range(0, terms, tile):
            product = dot(lhs, wk[t:t + tile], ((1,), (1,)))
            yield t, halves(slab[rows, t:t + tile] / product)

    def doc_partial(h, c, out):
        both, one = None, None
        for t, (high, low) in quotients(h, slice(c * chunk, (c + 1) * chunk)):
            b = dot(high, wk[t:t + tile, rank:])
            o = dot(low, wk[t:t + tile, :rank])
            both, one = (b, o) if both is None else (both + b, one + o)
        out[...] = both[:, :rank] + both[:, rank:] + one

    def term_partial(h, c):
        high_t, low_t = halves(h.T)
        lhs = jnp.concatenate([high_t, low_t], axis=0)
        for t, (high, low) in quotients(h, slice(c * chunk, (c + 1) * chunk)):
            b = dot(lhs, high)
            value = b[:rank] + b[rank:] + dot(high_t, low)
            if c > 0:
                value = value + tt[:, t:t + tile]
            tt[:, t:t + tile] = value

    for o in range(OUTER):
        w_old = w_in if o == 0 else wbuf.at[o - 1]
        w_new = w_out if o == OUTER - 1 else wbuf.at[o]
        w = w_old[...]
        high, low = halves(w)
        wk[:, :rank] = high
        wk[:, rank:2 * rank] = high
        wk[:, 2 * rank:] = low
        mass = Mass(gt, mbuf.at[o], mgot.at[o], msend.at[o], mrecv.at[o])
        mass.s1(fold(w))

        def h_ref(u):
            if u == 0:
                return h_in
            return h_out if u == OUTER * INNER else hbuf.at[u - 1]

        jobs = []
        count = INNER * DOC_CHUNKS
        doc_mass = None
        for j in range(count + DOC_CHUNKS):
            u, c = o * INNER + j // DOC_CHUNKS, j % DOC_CHUNKS
            rows = slice(c * chunk, (c + 1) * chunk)
            if j >= DOC_CHUNKS:
                jobs[j - DOC_CHUNKS].s5()
            h = h_ref(u)[rows]
            if j < count:
                doc_partial(h, c, dpart.at[u, c])
                job = Reduce(gt, chunk, dpart.at[u, c], dr1.at[u, c], dacc.at[u, c], dr2.at[u, c],
                             dsend.at[u, c], drecv.at[u, c])
                job.u, job.c = u, c
                jobs.append(job)
                job.s1()
            else:
                doc_mass = fold(h) if doc_mass is None else doc_mass + fold(h)
                term_partial(h, c)
            if j == 1:
                mass.s2()
            if j == 2:
                mass.s3()
            if 1 <= j <= count:
                jobs[j - 1].s2()
            if 2 <= j <= count + 1:
                k = jobs[j - 2]
                k.s3(k.c * chunk, h_ref(k.u), h_ref(k.u + 1), mass.value)
            if 3 <= j <= count + 2:
                jobs[j - 3].s4()

        sums = Mass(gd, cbuf.at[o], cgot.at[o], csend.at[o], crecv.at[o])
        sums.s1(doc_mass)
        jobs = []
        for c in range(TERM_CHUNKS):
            tpart[o, c] = tt[:, c * tchunk:(c + 1) * tchunk].T
            job = Reduce(gd, tchunk, tpart.at[o, c], tr1.at[o, c], tacc.at[o, c], tr2.at[o, c],
                         tsend.at[o, c], trecv.at[o, c])
            jobs.append(job)
            job.s1()
        sums.s2()
        for job in jobs:
            job.s2()
        sums.s3()
        for c, job in enumerate(jobs):
            job.s3(c * tchunk, w_old, w_new, sums.value)
        for job in jobs:
            job.s4()
        for job in jobs:
            job.s5()


def solution(mesh):
    n, m = mesh.shape["term"], mesh.shape["doc"]

    def on_device(slab, h, w):
        docs, rank = h.shape
        terms = w.shape[0]
        chunk, tchunk = docs // DOC_CHUNKS, terms // TERM_CHUNKS
        vmem = pl.BlockSpec(memory_space=pltpu.VMEM)
        updates = OUTER * INNER

        def reduce_scratch(lead, rows, size):
            outer = size // 2
            half = rows // 2
            return [
                pltpu.VMEM(lead + (rows, rank), F32),
                pltpu.VMEM(lead + (half, rank), F32),
                pltpu.VMEM(lead + (half, rank), F32),
                pltpu.VMEM(lead + (max(outer - 1, 1), half // outer, rank), F32),
                pltpu.SemaphoreType.DMA(lead + (4,)),
                pltpu.SemaphoreType.DMA(lead + (4,)),
            ]

        def mass_scratch(size):
            return [
                pltpu.VMEM((OUTER, 3, 8, rank), F32),
                pltpu.VMEM((OUTER, size // 2, 8, rank), F32),
                pltpu.SemaphoreType.DMA((OUTER, 2)),
                pltpu.SemaphoreType.DMA((OUTER, 2)),
            ]

        return pl.pallas_call(
            functools.partial(kernel, ("doc", m), ("term", n)),
            out_shape=[jax.ShapeDtypeStruct(h.shape, F32), jax.ShapeDtypeStruct(w.shape, F32)],
            in_specs=[vmem] * 3,
            out_specs=[vmem] * 2,
            scratch_shapes=[
                pltpu.VMEM((updates - 1, docs, rank), F32),
                pltpu.VMEM((max(OUTER - 1, 1), terms, rank), F32),
                pltpu.VMEM((terms, 3 * rank), BF16),
                pltpu.VMEM((rank, terms), F32),
                *reduce_scratch((updates, DOC_CHUNKS), chunk, n),
                *reduce_scratch((OUTER, TERM_CHUNKS), tchunk, m),
                *mass_scratch(n),
                *mass_scratch(m),
            ],
            compiler_params=pltpu.CompilerParams(
                collective_id=0, has_side_effects=True, vmem_limit_bytes=56 * 1024 * 1024),
            cost_estimate=pl.CostEstimate(
                flops=36 * 2 * docs * terms * rank, bytes_accessed=6 * docs * terms, transcendentals=0),
        )(slab, h, w)

    return jax.shard_map(
        on_device,
        mesh=mesh,
        in_specs=(P("doc", "term"), P("doc", None), P("term", None)),
        out_specs=(P("doc", None), P("term", None)),
        check_vma=False,
    )
```

time: 440 us -> 145 us (0.33); the launches traced: 434 us -> 144 us
  waiting for transfers between devices: 299 us -> 0 us
  Pallas kernels: 0 us -> 140 us
  blocking collectives: 57 us -> 0 us
  matrix products: 56.7 us -> 0 us
  between operations: 14.5 us -> 0.64 us
  other arithmetic: 6.1 us -> 0 us
    psum x6 -> x0, waiting for transfers between devices: 299 us -> none  [the longest x4 245 us: on_device(): numerator = lax.psum(partial_value, 'term')]
    pallas_call x0 -> x1, Pallas kernels: none -> 140 us  [on_device(): pl.pallas_call(functools.partial(kernel, ('doc', m), ('term', n)), out_sh...]
    psum x4 -> x0, blocking collectives: 57 us -> none  [the longest x2 45.2 us: on_device(): term_mass = lax.psum(jnp.sum(term_factor, axis=0), 'term')]
    dot_general x12 -> x0, matrix products: 56.7 us -> none  [the longest x6 24.6 us: quotient(): jnp.dot(doc_factor, term_factor.T, precision=lax.Precision.HIGHEST, prefe...]
  transfers between devices with their start and end apart: 6 -> 0, of which waited for: 6 -> 0; matrix products, arithmetic and copies ran while one was open for 0% -> 0% of each run, Pallas kernels for 0% -> 0%
where the time goes in v1:
time: 145 us; the launch traced here: 144 us
  Pallas kernels  140 us (97%)
  local copies, waits for them, and re-layouts  3.74 us (3%)
    pallas_call x1, Pallas kernels, on_device(): pl.pallas_call(functools.partial(kernel, ('doc', m), ('term', n)), out_sh...  140 us
    unnamed x2, local copies, waits for them, and re-layouts  3.74 us

profile of v1, /device:TPU:0, one launch (start us, length us, event | category | flops | bytes accessed | tf_op | source)
XLA Modules:
  0.0 144.5 jit_solution(371582518812510933)
XLA Ops:
  0.6 140.1 %shard_map.50 = (f32[1024,128]{1,0:T(8,128)}, f32[1024,128]{1,0:T(8,128)}) custom-call(f32[1024,1024]{1,0:T(8,128)} %slab.1, f32[1024,128]{1,0:T(8,128)} %h_in.1, f32[1024,128]{1,0:T(8,128)} %w_in.1), custom_call_target="tpu_custom_call" | custom-call | flops 9663676416 | bytes 6291456 | tf_op jit(solution)/shard_map/pallas_call | solution.py:283
  140.8 1.9 %copy.7 = f32[1024,128]{1,0:T(8,128)} copy(f32[1024,128]{1,0:T(8,128)} %get-tuple-element.4) | data formatting | bytes 1048576
  142.6 1.9 %copy.8 = f32[1024,128]{1,0:T(8,128)} copy(f32[1024,128]{1,0:T(8,128)} %get-tuple-element.5) | data formatting | bytes 1048576

commit v2 on v1

--- a/solution.py
+++ b/solution.py
@@ -9,9 +9,8 @@
 
 OUTER = 2
 INNER = 2
-TILE = 256
-DOC_CHUNKS = 4
-TERM_CHUNKS = 2
+DOC_CHUNKS = 8
+TERM_CHUNKS = 4
 MESH = pl.DeviceIdType.MESH
 F32 = jnp.float32
 BF16 = jnp.bfloat16
@@ -140,7 +139,7 @@
         return self.buf[2, 0:1]
 
 
-def kernel(docs_axis, terms_axis, slab, h_in, w_in, h_out, w_out,
+def kernel(docs_axis, terms_axis, doc_chunks, term_chunks, slab, h_in, w_in, h_out, w_out,
            hbuf, wbuf, wk, tt,
            dpart, dr1, dacc, dr2, dsend, drecv,
            tpart, tr1, tacc, tr2, tsend, trecv,
@@ -154,61 +153,75 @@
         pl.semaphore_signal(barrier, inc=1, device_id=device, device_id_type=MESH)
     pl.semaphore_wait(barrier, len(peers))
 
-    chunk, tchunk = docs // DOC_CHUNKS, terms // TERM_CHUNKS
-    tile = min(TILE, terms)
-
-    def quotients(h, rows):
+    chunk, tchunk = docs // doc_chunks, terms // term_chunks
+
+    def split_terms(w, t):
+        rows = slice(t * tchunk, (t + 1) * tchunk)
+        high, low = halves(w)
+        wk[rows, :rank] = high
+        wk[rows, rank:2 * rank] = high
+        wk[rows, 2 * rank:] = low
+
+    def quotients(h, c, t):
         high, low = halves(h)
         lhs = jnp.concatenate([high, low, high], axis=1)
-        for t in range(0, terms, tile):
-            product = dot(lhs, wk[t:t + tile], ((1,), (1,)))
-            yield t, halves(slab[rows, t:t + tile] / product)
-
-    def doc_partial(h, c, out):
+        rows, cols = slice(c * chunk, (c + 1) * chunk), slice(t * tchunk, (t + 1) * tchunk)
+        product = dot(lhs, wk[cols], ((1,), (1,)))
+        return halves(slab[rows, cols] / product)
+
+    def doc_partial(h, c, tiles, out):
         both, one = None, None
-        for t, (high, low) in quotients(h, slice(c * chunk, (c + 1) * chunk)):
-            b = dot(high, wk[t:t + tile, rank:])
-            o = dot(low, wk[t:t + tile, :rank])
+        for t in tiles:
+            high, low = quotients(h, c, t)
+            cols = slice(t * tchunk, (t + 1) * tchunk)
+            b = dot(high, wk[cols, rank:])
+            o = dot(low, wk[cols, :rank])
             both, one = (b, o) if both is None else (both + b, one + o)
-        out[...] = both[:, :rank] + both[:, rank:] + one
-
-    def term_partial(h, c):
+        value = both[:, :rank] + both[:, rank:] + one
+        out[...] = value if tiles[0] == 0 else out[...] + value
+
+    def term_partial(h, c, t):
         high_t, low_t = halves(h.T)
-        lhs = jnp.concatenate([high_t, low_t], axis=0)
-        for t, (high, low) in quotients(h, slice(c * chunk, (c + 1) * chunk)):
-            b = dot(lhs, high)
-            value = b[:rank] + b[rank:] + dot(high_t, low)
-            if c > 0:
-                value = value + tt[:, t:t + tile]
-            tt[:, t:t + tile] = value
-
+        lhs = jnp.concatenate([high_t, low_t, high_t], axis=1)
+        high, low = quotients(h, c, t)
+        value = dot(lhs, jnp.concatenate([high, high, low], axis=0))
+        cols = slice(t * tchunk, (t + 1) * tchunk)
+        if c > 0:
+            value = value + tt[:, cols]
+        if c < doc_chunks - 1:
+            tt[:, cols] = value
+        return value
+
+    def w_ref(o):
+        if o == 0:
+            return w_in
+        return w_out if o == OUTER else wbuf.at[o - 1]
+
+    def h_ref(u):
+        if u == 0:
+            return h_in
+        return h_out if u == OUTER * INNER else hbuf.at[u - 1]
+
+    tiles = list(range(term_chunks))
+    count = INNER * doc_chunks
+    lag = max(doc_chunks // 4, 1)
+    for t in tiles:
+        split_terms(w_in[t * tchunk:(t + 1) * tchunk], t)
+    term_mass = fold(w_in[...])
     for o in range(OUTER):
-        w_old = w_in if o == 0 else wbuf.at[o - 1]
-        w_new = w_out if o == OUTER - 1 else wbuf.at[o]
-        w = w_old[...]
-        high, low = halves(w)
-        wk[:, :rank] = high
-        wk[:, rank:2 * rank] = high
-        wk[:, 2 * rank:] = low
         mass = Mass(gt, mbuf.at[o], mgot.at[o], msend.at[o], mrecv.at[o])
-        mass.s1(fold(w))
-
-        def h_ref(u):
-            if u == 0:
-                return h_in
-            return h_out if u == OUTER * INNER else hbuf.at[u - 1]
-
-        jobs = []
-        count = INNER * DOC_CHUNKS
+        mass.s1(term_mass)
+        sums = Mass(gd, cbuf.at[o], cgot.at[o], csend.at[o], crecv.at[o])
+
+        jobs, term_jobs = [], []
         doc_mass = None
-        for j in range(count + DOC_CHUNKS):
-            u, c = o * INNER + j // DOC_CHUNKS, j % DOC_CHUNKS
-            rows = slice(c * chunk, (c + 1) * chunk)
-            if j >= DOC_CHUNKS:
-                jobs[j - DOC_CHUNKS].s5()
-            h = h_ref(u)[rows]
+        for j in range(count + doc_chunks):
+            u, c = o * INNER + j // doc_chunks, j % doc_chunks
+            if j >= doc_chunks:
+                jobs[j - doc_chunks].s5()
+            h = h_ref(u)[c * chunk:(c + 1) * chunk]
             if j < count:
-                doc_partial(h, c, dpart.at[u, c])
+                doc_partial(h, c, tiles[-1:] if o > 0 and j < doc_chunks else tiles, dpart.at[u, c])
                 job = Reduce(gt, chunk, dpart.at[u, c], dr1.at[u, c], dacc.at[u, c], dr2.at[u, c],
                              dsend.at[u, c], drecv.at[u, c])
                 job.u, job.c = u, c
@@ -216,38 +229,48 @@
                 job.s1()
             else:
                 doc_mass = fold(h) if doc_mass is None else doc_mass + fold(h)
-                term_partial(h, c)
+                if c == doc_chunks - 1:
+                    sums.s1(doc_mass)
+                for t in tiles:
+                    value = term_partial(h, c, t)
+                    if c == doc_chunks - 1:
+                        tpart[o, t] = value.T
+                        job = Reduce(gd, tchunk, tpart.at[o, t], tr1.at[o, t], tacc.at[o, t], tr2.at[o, t],
+                                     tsend.at[o, t], trecv.at[o, t])
+                        term_jobs.append(job)
+                        job.s1()
             if j == 1:
                 mass.s2()
             if j == 2:
                 mass.s3()
-            if 1 <= j <= count:
-                jobs[j - 1].s2()
-            if 2 <= j <= count + 1:
-                k = jobs[j - 2]
+            if 0 <= j - lag < count:
+                jobs[j - lag].s2()
+            if 0 <= j - 2 * lag < count:
+                k = jobs[j - 2 * lag]
                 k.s3(k.c * chunk, h_ref(k.u), h_ref(k.u + 1), mass.value)
-            if 3 <= j <= count + 2:
-                jobs[j - 3].s4()
-
-        sums = Mass(gd, cbuf.at[o], cgot.at[o], csend.at[o], crecv.at[o])
-        sums.s1(doc_mass)
-        jobs = []
-        for c in range(TERM_CHUNKS):
-            tpart[o, c] = tt[:, c * tchunk:(c + 1) * tchunk].T
-            job = Reduce(gd, tchunk, tpart.at[o, c], tr1.at[o, c], tacc.at[o, c], tr2.at[o, c],
-                         tsend.at[o, c], trecv.at[o, c])
-            jobs.append(job)
-            job.s1()
+            if 0 <= j - 3 * lag < count:
+                jobs[j - 3 * lag].s4()
+
         sums.s2()
-        for job in jobs:
+        for job in term_jobs:
             job.s2()
         sums.s3()
-        for c, job in enumerate(jobs):
-            job.s3(c * tchunk, w_old, w_new, sums.value)
-        for job in jobs:
+        for t, job in enumerate(term_jobs):
+            job.s3(t * tchunk, w_ref(o), w_ref(o + 1), sums.value)
+        for job in term_jobs:
             job.s4()
-        for job in jobs:
+        term_mass = None
+        for t, job in enumerate(term_jobs):
             job.s5()
+            if o == OUTER - 1:
+                continue
+            w = w_ref(o + 1)[t * tchunk:(t + 1) * tchunk]
+            term_mass = fold(w) if term_mass is None else term_mass + fold(w)
+            split_terms(w, t)
+            if t < term_chunks - 1:
+                u = (o + 1) * INNER
+                for c in range(doc_chunks):
+                    doc_partial(h_ref(u)[c * chunk:(c + 1) * chunk], c, [t], dpart.at[u, c])
 
 
 def solution(mesh):
@@ -256,7 +279,9 @@
     def on_device(slab, h, w):
         docs, rank = h.shape
         terms = w.shape[0]
-        chunk, tchunk = docs // DOC_CHUNKS, terms // TERM_CHUNKS
+        doc_chunks = min(DOC_CHUNKS, docs // (8 * n))
+        term_chunks = min(TERM_CHUNKS, terms // (8 * m))
+        chunk, tchunk = docs // doc_chunks, terms // term_chunks
         vmem = pl.BlockSpec(memory_space=pltpu.VMEM)
         updates = OUTER * INNER
 
@@ -281,7 +306,7 @@
             ]
 
         return pl.pallas_call(
-            functools.partial(kernel, ("doc", m), ("term", n)),
+            functools.partial(kernel, ("doc", m), ("term", n), doc_chunks, term_chunks),
             out_shape=[jax.ShapeDtypeStruct(h.shape, F32), jax.ShapeDtypeStruct(w.shape, F32)],
             in_specs=[vmem] * 3,
             out_specs=[vmem] * 2,
@@ -290,8 +315,8 @@
                 pltpu.VMEM((max(OUTER - 1, 1), terms, rank), F32),
                 pltpu.VMEM((terms, 3 * rank), BF16),
                 pltpu.VMEM((rank, terms), F32),
-                *reduce_scratch((updates, DOC_CHUNKS), chunk, n),
-                *reduce_scratch((OUTER, TERM_CHUNKS), tchunk, m),
+                *reduce_scratch((updates, doc_chunks), chunk, n),
+                *reduce_scratch((OUTER, term_chunks), tchunk, m),
                 *mass_scratch(n),
                 *mass_scratch(m),
             ],

time: 145 us -> 143 us (0.986)
    pallas_call x1, Pallas kernels: 140 us -> 139 us  [on_device(): pl.pallas_call(functools.partial(kernel, ('doc', m), ('term', n), doc_chu...]
where the time goes in v2:
time: 143 us
  Pallas kernels  139 us (97%)
  local copies, waits for them, and re-layouts  3.74 us (3%)
    pallas_call x1, Pallas kernels, on_device(): pl.pallas_call(functools.partial(kernel, ('doc', m), ('term', n), doc_chu...  139 us
    unnamed x2, local copies, waits for them, and re-layouts  3.74 us

profile of v2, /device:TPU:0, one launch (start us, length us, event | category | flops | bytes accessed | tf_op | source)
XLA Modules:
  0.0 143.0 jit_solution(7202720629869378137)
XLA Ops:
  0.6 138.7 %shard_map.50 = (f32[1024,128]{1,0:T(8,128)}, f32[1024,128]{1,0:T(8,128)}) custom-call(f32[1024,1024]{1,0:T(8,128)} %slab.1, f32[1024,128]{1,0:T(8,128)} %h_in.1, f32[1024,128]{1,0:T(8,128)} %w_in.1), custom_call_target="tpu_custom_call" | custom-call | flops 9663676416 | bytes 6291456 | tf_op jit(solution)/shard_map/pallas_call | solution.py:308
  139.3 1.9 %copy.7 = f32[1024,128]{1,0:T(8,128)} copy(f32[1024,128]{1,0:T(8,128)} %get-tuple-element.4) | data formatting | bytes 1048576
  141.2 1.9 %copy.8 = f32[1024,128]{1,0:T(8,128)} copy(f32[1024,128]{1,0:T(8,128)} %get-tuple-element.5) | data formatting | bytes 1048576

commit v3 on v2

--- a/solution.py
+++ b/solution.py
@@ -9,7 +9,7 @@
 
 OUTER = 2
 INNER = 2
-DOC_CHUNKS = 8
+DOC_CHUNKS = 4
 TERM_CHUNKS = 4
 MESH = pl.DeviceIdType.MESH
 F32 = jnp.float32
@@ -25,34 +25,40 @@
     return lax.dot_general(a, b, (dims, ((), ())), preferred_element_type=F32)
 
 
+def inverse(x):
+    y = pl.reciprocal(x, approx=True)
+    return y * (2.0 - x * y)
+
+
 def fold(x):
     rows, cols = x.shape
     return jnp.sum(x.reshape(rows // 8, 8, cols), axis=0)
 
 
 class Group:
-    def __init__(self, axis, size):
-        self.axis, self.size = axis, size
-        self.outer = size // 2
+    def __init__(self, axis, size, inner):
+        self.axis, self.inner = axis, inner
+        self.outer = size // inner
         self.me = lax.axis_index(axis)
-        self.x = lax.rem(self.me, 2)
-        self.z = lax.div(self.me, 2)
-        self.pair = {axis: self.me + 1 - 2 * self.x}
+        self.x = lax.rem(self.me, inner)
+        self.z = lax.div(self.me, inner)
+        self.pair = {axis: self.me + 1 - 2 * self.x} if inner == 2 else None
 
     def place(self, d):
         return lax.rem(self.z + d, self.outer)
 
     def peer(self, d):
-        return {self.axis: self.place(d) * 2 + self.x}
+        return {self.axis: self.place(d) * self.inner + self.x}
 
     def everyone(self):
-        return [self.pair] + [self.peer(d) for d in range(1, self.outer)]
+        return ([self.pair] if self.pair else []) + [self.peer(d) for d in range(1, self.outer)]
 
 
 class Reduce:
     def __init__(self, group, rows, part, r1, acc, r2, send, recv):
         self.g, self.rows = group, rows
-        self.half, self.own = rows // 2, rows // 2 // group.outer
+        self.half = rows // group.inner
+        self.own = self.half // group.outer
         self.part, self.r1, self.acc, self.r2 = part, r1, acc, r2
         self.send, self.recv = send, recv
 
@@ -68,12 +74,21 @@
         return pl.multiple_of(x * self.half, 8)
 
     def s1(self):
+        if self.g.inner == 1:
+            self.acc = self.part
+            self.scatter()
+            return
         self.c1 = self.copy(self.part.at[pl.ds(self.half_at(1 - self.g.x), self.half)], self.r1, 0, self.g.pair)
         self.c1.start()
 
     def s2(self):
+        if self.g.inner == 1:
+            return
         self.c1.wait()
         self.acc[...] = self.part[pl.ds(self.half_at(self.g.x), self.half)] + self.r1[...]
+        self.scatter()
+
+    def scatter(self):
         for d in range(1, self.g.outer):
             at = pl.multiple_of(self.g.place(d) * self.own, 8)
             self.copy(self.acc.at[pl.ds(at, self.own)], self.r2.at[d - 1], 1, self.g.peer(d)).start()
@@ -92,6 +107,8 @@
             self.copy(new.at[rows], new.at[rows], 2, self.g.peer(d)).start()
 
     def s4(self):
+        if self.g.inner == 1:
+            return
         if self.g.outer > 1:
             self.many(self.recv.at[2])
             self.many(self.send.at[1])
@@ -100,7 +117,11 @@
         self.c4.start()
 
     def s5(self):
-        self.c4.wait()
+        if self.g.inner == 2:
+            self.c4.wait()
+        else:
+            self.many(self.recv.at[2])
+            self.many(self.send.at[1])
         if self.g.outer > 1:
             self.many(self.send.at[2])
 
@@ -116,12 +137,21 @@
 
     def s1(self, value):
         self.buf[0] = value
+        if self.g.inner == 1:
+            self.buf[1] = value
+            self.scatter()
+            return
         self.c1 = self.copy(self.buf.at[0], self.got.at[0], 0, self.g.pair)
         self.c1.start()
 
     def s2(self):
+        if self.g.inner == 1:
+            return
         self.c1.wait()
         self.buf[1] = self.buf[0] + self.got[0]
+        self.scatter()
+
+    def scatter(self):
         for d in range(1, self.g.outer):
             self.copy(self.buf.at[1], self.got.at[d], 1, self.g.peer(d)).start()
 
@@ -146,7 +176,7 @@
            mbuf, mgot, msend, mrecv, cbuf, cgot, csend, crecv):
     docs, terms = slab.shape
     rank = h_in.shape[1]
-    gt, gd = Group(*terms_axis), Group(*docs_axis)
+    gt, gd = Group(*terms_axis, 1), Group(*docs_axis, 2)
     peers = gt.everyone() + gd.everyone()
     barrier = pltpu.get_barrier_semaphore()
     for device in peers:
@@ -167,7 +197,7 @@
         lhs = jnp.concatenate([high, low, high], axis=1)
         rows, cols = slice(c * chunk, (c + 1) * chunk), slice(t * tchunk, (t + 1) * tchunk)
         product = dot(lhs, wk[cols], ((1,), (1,)))
-        return halves(slab[rows, cols] / product)
+        return halves(slab[rows, cols] * inverse(product))
 
     def doc_partial(h, c, tiles, out):
         both, one = None, None
@@ -204,7 +234,7 @@
 
     tiles = list(range(term_chunks))
     count = INNER * doc_chunks
-    lag = max(doc_chunks // 4, 1)
+    lag = max(doc_chunks // 2, 1)
     for t in tiles:
         split_terms(w_in[t * tchunk:(t + 1) * tchunk], t)
     term_mass = fold(w_in[...])
@@ -240,16 +270,10 @@
                         term_jobs.append(job)
                         job.s1()
             if j == 1:
-                mass.s2()
-            if j == 2:
                 mass.s3()
             if 0 <= j - lag < count:
-                jobs[j - lag].s2()
-            if 0 <= j - 2 * lag < count:
-                k = jobs[j - 2 * lag]
+                k = jobs[j - lag]
                 k.s3(k.c * chunk, h_ref(k.u), h_ref(k.u + 1), mass.value)
-            if 0 <= j - 3 * lag < count:
-                jobs[j - 3 * lag].s4()
 
         sums.s2()
         for job in term_jobs:
@@ -285,22 +309,22 @@
         vmem = pl.BlockSpec(memory_space=pltpu.VMEM)
         updates = OUTER * INNER
 
-        def reduce_scratch(lead, rows, size):
-            outer = size // 2
-            half = rows // 2
+        def reduce_scratch(lead, rows, size, inner):
+            outer, half = size // inner, rows // inner
+            near = half if inner == 2 else 8
             return [
                 pltpu.VMEM(lead + (rows, rank), F32),
-                pltpu.VMEM(lead + (half, rank), F32),
-                pltpu.VMEM(lead + (half, rank), F32),
+                pltpu.VMEM(lead + (near, rank), F32),
+                pltpu.VMEM(lead + (near, rank), F32),
                 pltpu.VMEM(lead + (max(outer - 1, 1), half // outer, rank), F32),
                 pltpu.SemaphoreType.DMA(lead + (4,)),
                 pltpu.SemaphoreType.DMA(lead + (4,)),
             ]
 
-        def mass_scratch(size):
+        def mass_scratch(size, inner):
             return [
                 pltpu.VMEM((OUTER, 3, 8, rank), F32),
-                pltpu.VMEM((OUTER, size // 2, 8, rank), F32),
+                pltpu.VMEM((OUTER, size // inner, 8, rank), F32),
                 pltpu.SemaphoreType.DMA((OUTER, 2)),
                 pltpu.SemaphoreType.DMA((OUTER, 2)),
             ]
@@ -315,10 +339,10 @@
                 pltpu.VMEM((max(OUTER - 1, 1), terms, rank), F32),
                 pltpu.VMEM((terms, 3 * rank), BF16),
                 pltpu.VMEM((rank, terms), F32),
-                *reduce_scratch((updates, doc_chunks), chunk, n),
-                *reduce_scratch((OUTER, term_chunks), tchunk, m),
-                *mass_scratch(n),
-                *mass_scratch(m),
+                *reduce_scratch((updates, doc_chunks), chunk, n, 1),
+                *reduce_scratch((OUTER, term_chunks), tchunk, m, 2),
+                *mass_scratch(n, 1),
+                *mass_scratch(m, 2),
             ],
             compiler_params=pltpu.CompilerParams(
                 collective_id=0, has_side_effects=True, vmem_limit_bytes=56 * 1024 * 1024),

time: 143 us -> 143 us (level)
  no operation moved by 1% of the time
where the time goes in v3:
time: 143 us
  Pallas kernels  139 us (97%)
  local copies, waits for them, and re-layouts  3.74 us (3%)
    pallas_call x1, Pallas kernels, on_device(): pl.pallas_call(functools.partial(kernel, ('doc', m), ('term', n), doc_chu...  139 us
    unnamed x2, local copies, waits for them, and re-layouts  3.74 us

profile of v3, /device:TPU:0, one launch (start us, length us, event | category | flops | bytes accessed | tf_op | source)
XLA Modules:
  0.0 143.2 jit_solution(9881708177333393078)
XLA Ops:
  0.6 138.8 %shard_map.50 = (f32[1024,128]{1,0:T(8,128)}, f32[1024,128]{1,0:T(8,128)}) custom-call(f32[1024,1024]{1,0:T(8,128)} %slab.1, f32[1024,128]{1,0:T(8,128)} %h_in.1, f32[1024,128]{1,0:T(8,128)} %w_in.1), custom_call_target="tpu_custom_call" | custom-call | flops 9663676416 | bytes 6291456 | tf_op jit(solution)/shard_map/pallas_call | solution.py:332
  139.5 1.9 %copy.7 = f32[1024,128]{1,0:T(8,128)} copy(f32[1024,128]{1,0:T(8,128)} %get-tuple-element.4) | data formatting | bytes 1048576
  141.3 1.9 %copy.8 = f32[1024,128]{1,0:T(8,128)} copy(f32[1024,128]{1,0:T(8,128)} %get-tuple-element.5) | data formatting | bytes 1048576

commit v4 on v2

v4 whole, which is shorter than its diff:
```python
import functools

import jax
import jax.numpy as jnp
from jax import lax
from jax.experimental import pallas as pl
from jax.experimental.pallas import tpu as pltpu
from jax.sharding import PartitionSpec as P

OUTER = 2
INNER = 2
DOC_CHUNKS = 8
TERM_CHUNKS = 4
MESH = pl.DeviceIdType.MESH
F32 = jnp.float32
BF16 = jnp.bfloat16


def halves(x):
    high = x.astype(BF16)
    return high, (x - high.astype(F32)).astype(BF16)


def dot(a, b, dims=((1,), (0,))):
    return lax.dot_general(a, b, (dims, ((), ())), preferred_element_type=F32)


def inverse(x):
    y = pl.reciprocal(x, approx=True)
    return y * (2.0 - x * y)


def fold(x):
    rows, cols = x.shape
    return jnp.sum(x.reshape(rows // 8, 8, cols), axis=0)


class Group:
    def __init__(self, axis, size):
        self.axis, self.size = axis, size
        self.outer = size // 2
        self.me = lax.axis_index(axis)
        self.x = lax.rem(self.me, 2)
        self.z = lax.div(self.me, 2)
        self.pair = {axis: self.me + 1 - 2 * self.x}

    def place(self, d):
        return lax.rem(self.z + d, self.outer)

    def peer(self, d):
        return {self.axis: self.place(d) * 2 + self.x}

    def everyone(self):
        return [self.pair] + [self.peer(d) for d in range(1, self.outer)]


class Reduce:
    def __init__(self, group, rows, scratch, index, base, old, new):
        self.g, self.rows, self.base, self.old, self.new = group, rows, base, old, new
        self.half, self.own = rows // 2, rows // 2 // group.outer
        self.part, self.r1, self.acc, self.r2, self.send, self.recv = [ref.at[index] for ref in scratch]

    def copy(self, src, dst, stage, device):
        return pltpu.make_async_remote_copy(
            src_ref=src, dst_ref=dst, send_sem=self.send.at[stage], recv_sem=self.recv.at[stage],
            device_id=device, device_id_type=MESH)

    def many(self, sem):
        pltpu.make_async_copy(self.r2, self.r2, sem).wait()

    def half_at(self, x):
        return pl.multiple_of(x * self.half, 8)

    def near(self):
        return self.copy(self.part.at[pl.ds(self.half_at(1 - self.g.x), self.half)], self.r1, 0, self.g.pair)

    def back(self):
        rows = pl.ds(pl.multiple_of(self.base + self.half_at(self.g.x), 8), self.half)
        return self.copy(self.new.at[rows], self.new.at[rows], 3, self.g.pair)

    def s1(self):
        self.near().start()

    def s2(self):
        self.near().wait()
        self.acc[...] = self.part[pl.ds(self.half_at(self.g.x), self.half)] + self.r1[...]
        for d in range(1, self.g.outer):
            at = pl.multiple_of(self.g.place(d) * self.own, 8)
            self.copy(self.acc.at[pl.ds(at, self.own)], self.r2.at[d - 1], 1, self.g.peer(d)).start()

    def s3(self, mass):
        if self.g.outer > 1:
            self.many(self.recv.at[1])
        total = self.acc[pl.ds(pl.multiple_of(self.g.z * self.own, 8), self.own)]
        for d in range(self.g.outer - 1):
            total = total + self.r2[d]
        at = pl.multiple_of(self.base + self.half_at(self.g.x) + self.g.z * self.own, 8)
        rows = pl.ds(at, self.own)
        self.new[rows] = self.old[rows] * total / mass()
        for d in range(1, self.g.outer):
            self.copy(self.new.at[rows], self.new.at[rows], 2, self.g.peer(d)).start()

    def s4(self):
        if self.g.outer > 1:
            self.many(self.recv.at[2])
            self.many(self.send.at[1])
        self.back().start()

    def s5(self):
        self.back().wait()
        if self.g.outer > 1:
            self.many(self.send.at[2])


class Mass:
    def __init__(self, group, buf, got, send, recv):
        self.g, self.buf, self.got, self.send, self.recv = group, buf, got, send, recv

    def copy(self, src, dst, stage, device):
        return pltpu.make_async_remote_copy(
            src_ref=src, dst_ref=dst, send_sem=self.send.at[stage], recv_sem=self.recv.at[stage],
            device_id=device, device_id_type=MESH)

    def s1(self, value):
        self.buf[0] = value
        self.near().start()

    def near(self):
        return self.copy(self.buf.at[0], self.got.at[0], 0, self.g.pair)

    def s2(self):
        self.near().wait()
        self.buf[1] = self.buf[0] + self.got[0]
        for d in range(1, self.g.outer):
            self.copy(self.buf.at[1], self.got.at[d], 1, self.g.peer(d)).start()

    def s3(self):
        total = self.buf[1]
        if self.g.outer > 1:
            rest = self.got.at[pl.ds(1, self.g.outer - 1)]
            pltpu.make_async_copy(rest, rest, self.recv.at[1]).wait()
            pltpu.make_async_copy(rest, rest, self.send.at[1]).wait()
            for d in range(1, self.g.outer):
                total = total + self.got[d]
        self.buf[2] = jnp.broadcast_to(jnp.sum(total, axis=0, keepdims=True), total.shape)

    def value(self):
        return self.buf[2, 0:1]


def kernel(docs_axis, terms_axis, doc_chunks, term_chunks, slab, h_in, w_in, h_out, w_out,
           hbuf, wbuf, wt, wk, tt, dm,
           dpart, dr1, dacc, dr2, dsend, drecv,
           tpart, tr1, tacc, tr2, tsend, trecv,
           mbuf, mgot, msend, mrecv, cbuf, cgot, csend, crecv):
    docs, terms = slab.shape
    rank = h_in.shape[1]
    gt, gd = Group(*terms_axis), Group(*docs_axis)
    peers = gt.everyone() + gd.everyone()
    barrier = pltpu.get_barrier_semaphore()
    for device in peers:
        pl.semaphore_signal(barrier, inc=1, device_id=device, device_id_type=MESH)
    pl.semaphore_wait(barrier, len(peers))

    chunk, tchunk = docs // doc_chunks, terms // term_chunks

    tiles = [slice(t * tchunk, (t + 1) * tchunk) for t in range(term_chunks)]

    def quotients(h, rows, cols):
        high, low = halves(h)
        lhs = jnp.concatenate([high, low, high], axis=1)
        return halves(slab[rows, cols] * inverse(dot(lhs, wt[:, cols])))

    def doc_partial(h, rows, out):
        both, one = None, None
        for cols in tiles:
            high, low = quotients(h, rows, cols)
            b = dot(high, wk[cols])
            o = dot(low, wk[cols, :rank])
            both, one = (b, o) if both is None else (both + b, one + o)
        out[...] = both[:, :rank] + both[:, rank:] + one

    def term_partial(h, rows):
        high_t, low_t = halves(h.T)
        lhs = jnp.concatenate([high_t, low_t, high_t], axis=1)
        for cols in tiles:
            high, low = quotients(h, rows, cols)
            tt[:, cols] += dot(lhs, jnp.concatenate([high, high, low], axis=0))

    count = INNER * doc_chunks
    lag = max(doc_chunks // 4, 1)
    hbuf[0] = h_in[...]
    wbuf[0] = w_in[...]

    def doc_job(q):
        u, c = lax.div(q, doc_chunks), lax.rem(q, doc_chunks)
        return Reduce(gt, chunk, (dpart, dr1, dacc, dr2, dsend, drecv), (u, c), c * chunk, hbuf.at[u], hbuf.at[u + 1])

    def outer(o, carry):
        mass = Mass(gt, mbuf.at[o], mgot.at[o], msend.at[o], mrecv.at[o])
        sums = Mass(gd, cbuf.at[o], cgot.at[o], csend.at[o], crecv.at[o])
        w_now, w_next = wbuf.at[o], wbuf.at[o + 1]
        mass.s1(fold(w_now[...]))
        for cols in tiles:
            high, low = halves(w_now[cols])
            wk[cols, :rank] = high
            wk[cols, rank:] = low
            high, low = halves(w_now[cols].T)
            wt[:rank, cols] = high
            wt[rank:2 * rank, cols] = high
            wt[2 * rank:, cols] = low
        tt[...] = jnp.zeros_like(tt)
        dm[...] = jnp.zeros_like(dm)

        def tick(j, carry):
            q = o * count + j
            u, c = lax.div(q, doc_chunks), lax.rem(q, doc_chunks)
            rows = pl.ds(pl.multiple_of(c * chunk, 8), chunk)

            @pl.when(j >= doc_chunks)
            def _():
                doc_job(q - doc_chunks).s5()

            @pl.when(j < count)
            def _():
                doc_partial(hbuf[u, rows], rows, dpart.at[u, c])
                doc_job(q).s1()

            @pl.when(j >= count)
            def _():
                h = hbuf[u, rows]
                dm[...] += fold(h)
                term_partial(h, rows)

            @pl.when(j == 1)
            def _():
                mass.s2()

            @pl.when(j == 2)
            def _():
                mass.s3()

            @pl.when(jnp.logical_and(j >= lag, j < count + lag))
            def _():
                doc_job(q - lag).s2()

            @pl.when(jnp.logical_and(j >= 2 * lag, j < count + 2 * lag))
            def _():
                doc_job(q - 2 * lag).s3(mass.value)

            @pl.when(jnp.logical_and(j >= 3 * lag, j < count + 3 * lag))
            def _():
                doc_job(q - 3 * lag).s4()

            return carry

        lax.fori_loop(0, count + doc_chunks, tick, 0)

        sums.s1(dm[...])
        jobs = []
        for t, cols in enumerate(tiles):
            tpart[o, t] = tt[:, cols].T
            jobs.append(Reduce(gd, tchunk, (tpart, tr1, tacc, tr2, tsend, trecv), (o, t), t * tchunk, w_now, w_next))
            jobs[-1].s1()
        sums.s2()
        for job in jobs:
            job.s2()
        sums.s3()
        for job in jobs:
            job.s3(sums.value)
        for job in jobs:
            job.s4()
        for job in jobs:
            job.s5()
        return carry

    lax.fori_loop(0, OUTER, outer, 0)
    h_out[...] = hbuf[OUTER * INNER]
    w_out[...] = wbuf[OUTER]


def solution(mesh):
    n, m = mesh.shape["term"], mesh.shape["doc"]

    def on_device(slab, h, w):
        docs, rank = h.shape
        terms = w.shape[0]
        doc_chunks = min(DOC_CHUNKS, docs // (8 * n))
        term_chunks = min(TERM_CHUNKS, terms // (8 * m))
        chunk, tchunk = docs // doc_chunks, terms // term_chunks
        vmem = pl.BlockSpec(memory_space=pltpu.VMEM)
        updates = OUTER * INNER

        def reduce_scratch(lead, rows, size):
            outer = size // 2
            half = rows // 2
            return [
                pltpu.VMEM(lead + (rows, rank), F32),
                pltpu.VMEM(lead + (half, rank), F32),
                pltpu.VMEM(lead + (half, rank), F32),
                pltpu.VMEM(lead + (max(outer - 1, 1), half // outer, rank), F32),
                pltpu.SemaphoreType.DMA(lead + (4,)),
                pltpu.SemaphoreType.DMA(lead + (4,)),
            ]

        def mass_scratch(size):
            return [
                pltpu.VMEM((OUTER, 3, 8, rank), F32),
                pltpu.VMEM((OUTER, size // 2, 8, rank), F32),
                pltpu.SemaphoreType.DMA((OUTER, 2)),
                pltpu.SemaphoreType.DMA((OUTER, 2)),
            ]

        return pl.pallas_call(
            functools.partial(kernel, ("doc", m), ("term", n), doc_chunks, term_chunks),
            out_shape=[jax.ShapeDtypeStruct(h.shape, F32), jax.ShapeDtypeStruct(w.shape, F32)],
            in_specs=[vmem] * 3,
            out_specs=[vmem] * 2,
            scratch_shapes=[
                pltpu.VMEM((updates + 1, docs, rank), F32),
                pltpu.VMEM((OUTER + 1, terms, rank), F32),
                pltpu.VMEM((3 * rank, terms), BF16),
                pltpu.VMEM((terms, 2 * rank), BF16),
                pltpu.VMEM((rank, terms), F32),
                pltpu.VMEM((8, rank), F32),
                *reduce_scratch((updates, doc_chunks), chunk, n),
                *reduce_scratch((OUTER, term_chunks), tchunk, m),
                *mass_scratch(n),
                *mass_scratch(m),
            ],
            compiler_params=pltpu.CompilerParams(
                collective_id=0, has_side_effects=True, vmem_limit_bytes=56 * 1024 * 1024),
            cost_estimate=pl.CostEstimate(
                flops=36 * 2 * docs * terms * rank, bytes_accessed=6 * docs * terms, transcendentals=0),
        )(slab, h, w)

    return jax.shard_map(
        on_device,
        mesh=mesh,
        in_specs=(P("doc", "term"), P("doc", None), P("term", None)),
        out_specs=(P("doc", None), P("term", None)),
        check_vma=False,
    )
```

time: 143 us -> 132 us (0.923)
  Pallas kernels: 139 us -> 128 us
    pallas_call x1, Pallas kernels: 139 us -> 128 us  [on_device(): pl.pallas_call(functools.partial(kernel, ('doc', m), ('term', n), doc_chu...]
where the time goes in v4:
time: 132 us
  Pallas kernels  128 us (97%)
  local copies, waits for them, and re-layouts  3.74 us (3%)
    pallas_call x1, Pallas kernels, on_device(): pl.pallas_call(functools.partial(kernel, ('doc', m), ('term', n), doc_chu...  128 us
    unnamed x2, local copies, waits for them, and re-layouts  3.74 us

profile of v4, /device:TPU:0, one launch (start us, length us, event | category | flops | bytes accessed | tf_op | source)
XLA Modules:
  0.0 132.2 jit_solution(8367432570510450368)
XLA Ops:
  0.6 127.8 %shard_map.50 = (f32[1024,128]{1,0:T(8,128)}, f32[1024,128]{1,0:T(8,128)}) custom-call(f32[1024,1024]{1,0:T(8,128)} %slab.1, f32[1024,128]{1,0:T(8,128)} %h_in.1, f32[1024,128]{1,0:T(8,128)} %w_in.1), custom_call_target="tpu_custom_call" | custom-call | flops 9663676416 | bytes 6291456 | tf_op jit(solution)/shard_map/pallas_call | solution.py:314
  128.5 1.9 %copy.7 = f32[1024,128]{1,0:T(8,128)} copy(f32[1024,128]{1,0:T(8,128)} %get-tuple-element.4) | data formatting | bytes 1048576
  130.3 1.9 %copy.8 = f32[1024,128]{1,0:T(8,128)} copy(f32[1024,128]{1,0:T(8,128)} %get-tuple-element.5) | data formatting | bytes 1048576

commit v5 on v4

--- a/solution.py
+++ b/solution.py
@@ -172,13 +172,13 @@
         return halves(slab[rows, cols] * inverse(dot(lhs, wt[:, cols])))
 
     def doc_partial(h, rows, out):
-        both, one = None, None
+        total = None
         for cols in tiles:
             high, low = quotients(h, rows, cols)
-            b = dot(high, wk[cols])
-            o = dot(low, wk[cols, :rank])
-            both, one = (b, o) if both is None else (both + b, one + o)
-        out[...] = both[:, :rank] + both[:, rank:] + one
+            both = dot(jnp.concatenate([high, low], axis=0), wk[cols])
+            value = both[:chunk, :rank] + (both[:chunk, rank:] + both[chunk:, :rank])
+            total = value if total is None else total + value
+        out[...] = total
 
     def term_partial(h, rows):
         high_t, low_t = halves(h.T)
@@ -279,6 +279,11 @@
     w_out[...] = wbuf[OUTER]
 
 
+def hand_over(a, b, a_out, b_out):
+    a_out[...] = a[...]
+    b_out[...] = b[...]
+
+
 def solution(mesh):
     n, m = mesh.shape["term"], mesh.shape["doc"]
 
@@ -311,9 +316,10 @@
                 pltpu.SemaphoreType.DMA((OUTER, 2)),
             ]
 
-        return pl.pallas_call(
+        outs = [jax.ShapeDtypeStruct(h.shape, F32), jax.ShapeDtypeStruct(w.shape, F32)]
+        results = pl.pallas_call(
             functools.partial(kernel, ("doc", m), ("term", n), doc_chunks, term_chunks),
-            out_shape=[jax.ShapeDtypeStruct(h.shape, F32), jax.ShapeDtypeStruct(w.shape, F32)],
+            out_shape=outs,
             in_specs=[vmem] * 3,
             out_specs=[vmem] * 2,
             scratch_shapes=[
@@ -333,6 +339,7 @@
             cost_estimate=pl.CostEstimate(
                 flops=36 * 2 * docs * terms * rank, bytes_accessed=6 * docs * terms, transcendentals=0),
         )(slab, h, w)
+        return pl.pallas_call(hand_over, out_shape=outs, in_specs=[vmem] * 2, out_specs=[vmem] * 2)(*results)
 
     return jax.shard_map(
         on_device,

time: 132 us -> 128 us (0.970)
  local copies, waits for them, and re-layouts: 3.74 us -> 0 us
    unnamed x2 -> x0, local copies, waits for them, and re-layouts: 3.74 us -> none
    pallas_call x1, Pallas kernels: 128 us -> 125 us  [on_device(): pl.pallas_call(functools.partial(kernel, ('doc', m), ('term', n), doc_chu...]
    pallas_call x0 -> x1, Pallas kernels: none -> 2.2 us  [on_device(): pl.pallas_call(hand_over, out_shape=outs, in_specs=[vmem] * 2, out_specs=...]
where the time goes in v5:
time: 128 us
  Pallas kernels  128 us (100%)
    pallas_call x1, Pallas kernels, on_device(): pl.pallas_call(functools.partial(kernel, ('doc', m), ('term', n), doc_chu...  125 us

profile of v5, /device:TPU:0, one launch (start us, length us, event | category | flops | bytes accessed | tf_op | source)
XLA Modules:
  0.0 128.1 jit_solution(2845007096954575355)
XLA Ops:
  0.6 125.3 %shard_map.50 = (f32[1024,128]{1,0:T(8,128)}, f32[1024,128]{1,0:T(8,128)}) custom-call(f32[1024,1024]{1,0:T(8,128)} %slab.1, f32[1024,128]{1,0:T(8,128)} %h_in.1, f32[1024,128]{1,0:T(8,128)} %w_in.1), custom_call_target="tpu_custom_call" | custom-call | flops 9663676416 | bytes 6291456 | tf_op jit(solution)/shard_map/pallas_call | solution.py:320
  125.9 2.2 %shard_map.51 = (f32[1024,128]{1,0:T(8,128)}, f32[1024,128]{1,0:T(8,128)}) custom-call(f32[1024,128]{1,0:T(8,128)} %get-tuple-element.4.a, f32[1024,128]{1,0:T(8,128)} %get-tuple-element.5.b), custom_call_target="tpu_custom_call" | custom-call | tf_op jit(solution)/shard_map/pallas_call | solution.py:342
